TPU v7x, 32 devices: a whole 2x2x4 slice. The times are simulated.
32 devices in a mesh: fsdp: 4 (over z), grp: 8 (over y, x, core).
Axes of the slice: x: 2, y: 2, z: 4, core: 2. Of those that a mesh axis runs over, the one named last changes fastest.
Arguments:
- grads: bfloat16 [16, 384, 2048], P('grp', 'fsdp')
- momentum: bfloat16 [16, 384, 2048], P('grp', 'fsdp'), may hold values from -6 to 6
- row_counts: int32 [16], P('grp'), may hold values from 128 to 384, as said below
Outputs:
- update: bfloat16 [16, 384, 2048], P('grp', 'fsdp')
- new_momentum: bfloat16 [16, 384, 2048], P('grp', 'fsdp')
Inputs may be any that keep to these rules, and one draw needn't show every extreme that they name: `row_counts`: each entry is one, two or three times 384 // 3, and some entry equals 384.
All inputs are finite; a program needn't handle non-finite values.
Results may differ from a plain program's by a relative error of at most 0.007.
Values may be sent and summed in bfloat16 or wider, within the bound.
A program may use at most 64 MiB of HBM per device.

v0:
```python
import jax
import jax.numpy as jnp
from jax import lax
from jax.sharding import PartitionSpec as P

ITERS = 2


first_coef = 3.4445
second_coef = -4.775
third_coef = 2.0315


def shifted(x, axis, by):
    size = lax.axis_size(axis)
    return lax.ppermute(x, axis, [(i, (i + by) % size) for i in range(size)])


def orthogonal(matrix, combine):
    frob = jnp.sqrt(combine(jnp.sum(jnp.square(matrix.astype(jnp.float32)))))
    current = (matrix.astype(jnp.float32) / (frob + 1e-07)).astype(jnp.bfloat16)
    for step in range(ITERS):
        partial_gram = jnp.dot(current, current.T, preferred_element_type=jnp.float32)
        gram = combine(partial_gram).astype(jnp.bfloat16)
        square = jnp.dot(gram, gram, preferred_element_type=jnp.float32)
        poly = (second_coef * gram.astype(jnp.float32) + third_coef * square).astype(jnp.bfloat16)
        current = (
            first_coef * current.astype(jnp.float32)
            + jnp.dot(poly, current, preferred_element_type=jnp.float32)
        ).astype(jnp.bfloat16)
    return current


def local(grads, momentum, row_counts):
    matrices, rows_here, width = grads.shape
    group_size = lax.axis_size("fsdp")
    offset = lax.axis_index("fsdp") * rows_here
    row_ids = offset + lax.broadcasted_iota(jnp.int32, (1, rows_here, 1), 1)
    live = row_ids < row_counts[:, None, None]
    graded = jnp.where(live, grads.astype(jnp.float32), 0.0)
    live_rows = jnp.sum(jnp.clip(row_counts - offset, 0, rows_here)).astype(jnp.float32)
    square_sum, row_total = lax.psum((jnp.sum(graded * graded), live_rows), ("fsdp", "grp"))
    clip = jnp.minimum(1.0, lax.rsqrt(square_sum / (row_total * width) + 1e-06))
    new_momentum = jnp.where(live, 0.95 * momentum.astype(jnp.float32) + clip * graded, 0.0).astype(
        jnp.bfloat16
    )
    half = width // 2
    distance = group_size // 2
    halves = jnp.concatenate([new_momentum[:, :, :half], new_momentum[:, :, half:]], axis=0)
    owned = lax.all_to_all(halves, "fsdp", split_axis=0, concat_axis=1, tiled=True)

    def pair_total(value):
        return value + shifted(value.astype(jnp.bfloat16), "fsdp", distance).astype(value.dtype)

    result = orthogonal(owned[0], pair_total)
    returned = lax.all_to_all(result[None], "fsdp", split_axis=1, concat_axis=0, tiled=True)
    final = jnp.concatenate([returned[:matrices], returned[matrices:]], axis=2)
    update = (0.2 * jnp.sqrt(jnp.float32(width)) * final.astype(jnp.float32)).astype(jnp.bfloat16)
    return (update, new_momentum)


def solution(mesh):
    placed = (P("grp", "fsdp", None), P("grp", "fsdp", None), P("grp"))
    return jax.shard_map(
        local,
        mesh=mesh,
        in_specs=placed,
        out_specs=(P("grp", "fsdp", None), P("grp", "fsdp", None)),
        check_vma=False,
    )
```

profile of v0, /device:TPU:0, one launch (start us, length us, event | category | flops | bytes accessed | tf_op | source)
XLA Modules:
  0.0 147.6 jit_solution(13540265730353842263)
XLA Ops:
  0.6 1.3 clamp_reduce_fusion
  1.9 0.7 broadcast_compare_fusion
  2.7 2.2 %multiply_reduce_fusion = f32[]{:T(128)} fusion(bf16[2,96,2048]{2,1,0:T(8,128)(2,1)} %param.3, pred[2,96]{1,0:T(4,128)(4,1)S(1)} %broadcast_compare_fusion), kind=kLoop, calls=%fused_computation.8 | loop fusion | flops 1572863 | bytes 786628 | tf_op jit(solution)/shard_map/reduce_sum | solution.py:42
  5.5 42.3 %all-reduce = (f32[]{:T(128)}, f32[]{:T(128)}) all-reduce(f32[]{:T(128)} %multiply_reduce_fusion, f32[]{:T(128)S(6)} %convert_element_type.86), channel_id=1, replica_groups=mesh['fsdp'=4,'grp'=8] {'fsdp','grp'}, use_global_device_ids=true, to_apply=%region_1.2 | all-reduce | flops 2 | bytes 16 | tf_op jit(solution)/shard_map/psum | solution.py:42
  49.2 1.8 %select_convert_fusion = bf16[2,96,2048]{2,1,0:T(8,128)(2,1)S(1)} fusion(bf16[2,96,2048]{2,1,0:T(8,128)(2,1)} %param.3, bf16[2,96,2048]{2,1,0:T(8,128)(2,1)} %param.4, f32[]{:T(128)S(6)} %min_shard_map.3, pred[2,96]{1,0:T(4,128)(4,1)S(1)} %broadcast_compare_fusion), kind=kLoop, calls=%fused_computation.7 | loop fusion | flops 3145728 | bytes 2359492 | tf_op jit(solution)/shard_map/convert_element_type | solution.py:44
  51.0 0.0 copy-start
  51.0 0.1 fusion.11
  51.1 0.1 pad_maximum_fusion
  51.2 0.7 copy-done
  51.9 22.9 %all_to_all.21 = bf16[4,96,1024]{2,1,0:T(8,128)(2,1)S(1)} all-to-all(bf16[4,96,1024]{2,1,0:T(8,128)(2,1)S(1)} %pad_maximum_fusion), channel_id=1, replica_groups=mesh['fsdp'=4,'grp'=8] {'fsdp'}, dimensions={0} | all-to-all | bytes 1572864 | tf_op jit(solution)/shard_map/all_to_all | solution.py:50
  74.8 1.0 fusion
  76.5 1.5 %collective-permute-start = (bf16[]{:T(256)}, bf16[]{:T(256)}, u32[]{:S(2)}, u32[]{:S(2)}) collective-permute-start(bf16[]{:T(256)} %convert_element_type.89), channel_id=1, source_target_pairs={{0,16},{8,24},{16,0},{24,8},{1,17},{9,25},{17,1},{25,9},{2,18},{10... | collective-permute-start | bytes 14 | tf_op jit(solution)/shard_map/ppermute | solution.py:16
  78.0 3.1 %collective-permute-done = bf16[]{:T(256)} collective-permute-done((bf16[]{:T(256)}, bf16[]{:T(256)}, u32[]{:S(2)}, u32[]{:S(2)}) %collective-permute-start) | collective-permute-done | bytes 34 | tf_op jit(solution)/shard_map/ppermute | solution.py:16
  82.3 0.2 fusion.1
  82.5 0.6 fusion.12
  83.1 0.2 collective-permute-start.1
  83.3 12.8 %collective-permute-done.1 = bf16[384,384]{1,0:T(8,128)(2,1)S(1)} collective-permute-done((bf16[384,384]{1,0:T(8,128)(2,1)S(1)}, bf16[384,384]{1,0:T(8,128)(2,1)S(1)}, u32[]{:S(2)}, u32[]{:S(2)}) %collective-permute-start.1) | collective-permute-done | bytes 294944 | tf_op jit(solution)/shard_map/ppermute | solution.py:16
  96.2 0.8 add_convert_fusion.1
  97.0 0.6 fusion.13
  97.6 0.1 collective-permute-start.2
  97.7 15.4 %collective-permute-done.2 = bf16[384,384]{1,0:T(8,128)(2,1)S(1)} collective-permute-done((bf16[384,384]{1,0:T(8,128)(2,1)S(1)}, bf16[384,384]{1,0:T(8,128)(2,1)S(1)}, u32[]{:S(2)}, u32[]{:S(2)}) %collective-permute-start.2) | collective-permute-done | bytes 294944 | tf_op jit(solution)/shard_map/ppermute | solution.py:16
  113.1 0.8 fusion.2
  114.0 1.2 copy.11
  115.2 0.5 broadcast.63
  115.7 5.2 %reduce.3 = bf16[384,1024]{1,0:T(8,128)(2,1)S(1)} reduce(bf16[384,1,1024]{2,1,0:T(2,128)(2,1)S(1)} %bitcast.21, bf16[]{:T(256)} %broadcast.63), dimensions={1}, to_apply=%bitcast.16.reduce_sub_computation | reduce | bytes 1572866
  120.9 0.6 reshape.63
  121.6 23.0 %all_to_all.22 = bf16[4,2,49152]{2,1,0:T(2,128)(2,1)S(1)} all-to-all(bf16[4,2,49152]{2,1,0:T(2,128)(2,1)S(1)} %reshape.63), channel_id=1, replica_groups=mesh['fsdp'=4,'grp'=8] {'fsdp'}, dimensions={0} | all-to-all | bytes 1572864 | tf_op jit(solution)/shard_map/all_to_all | solution.py:56
  144.5 0.7 reshape.64
  145.3 0.8 slice.27
  146.1 0.3 copy.8
  146.4 0.1 copy.9
  146.6 1.0 multiply_convert_fusion
  (2 shorter events, 0.0 us)
Async XLA Ops:
  51.0 0.9 copy-start
  76.5 4.6 %collective-permute-start = (bf16[]{:T(256)}, bf16[]{:T(256)}, u32[]{:S(2)}, u32[]{:S(2)}) collective-permute-start(bf16[]{:T(256)} %convert_element_type.89), channel_id=1, source_target_pairs={{0,16},{8,24},{16,0},{24,8},{1,17},{9,25},{17,1},{25,9},{2,18},{10... | collective-permute-start | bytes 14 | tf_op jit(solution)/shard_map/ppermute | solution.py:16
  83.1 13.1 %collective-permute-start.1 = (bf16[384,384]{1,0:T(8,128)(2,1)S(1)}, bf16[384,384]{1,0:T(8,128)(2,1)S(1)}, u32[]{:S(2)}, u32[]{:S(2)}) collective-permute-start(bf16[384,384]{1,0:T(8,128)(2,1)S(1)} %get-tuple-element.6), channel_id=1, source_target_pairs={{0,16},{8,24},{16,0},{24,8},{1,17},{9,25},{17,1},{25,9},{2,18},{10... | collective-permute-start | bytes 884744 | tf_op jit(solution)/shard_map/ppermute | solution.py:16
  97.6 15.5 %collective-permute-start.2 = (bf16[384,384]{1,0:T(8,128)(2,1)S(1)}, bf16[384,384]{1,0:T(8,128)(2,1)S(1)}, u32[]{:S(2)}, u32[]{:S(2)}) collective-permute-start(bf16[384,384]{1,0:T(8,128)(2,1)S(1)} %get-tuple-element.8), channel_id=1, source_target_pairs={{0,16},{8,24},{16,0},{24,8},{1,17},{9,25},{17,1},{25,9},{2,18},{10... | collective-permute-start | bytes 884744 | tf_op jit(solution)/shard_map/ppermute | solution.py:16
where the time goes:
time: 148 us
  blocking collectives  88.2 us (60%)
  waiting for transfers between devices  31.3 us (21%)
  other arithmetic  13.6 us (9%)
  local copies, waits for them, and re-layouts  5.12 us (3%)
  between operations  4.69 us (3%)
  matrix products  2.87 us (2%)
  starting transfers between devices  1.83 us (1%)
    psum x1, blocking collectives, local(): lax.psum((jnp.sum(graded * graded), live_rows), ('fsdp', 'grp'))  42.3 us
    ppermute x3, waiting for transfers between devices, shifted(): return lax.ppermute(x, axis, [(i, (i + by) % size) for i in range(size)])  31.3 us
    all_to_all x1, blocking collectives, local(): lax.all_to_all(result[None], 'fsdp', split_axis=1, concat_axis=0, tiled=T...  23 us
    all_to_all x1, blocking collectives, local(): lax.all_to_all(halves, 'fsdp', split_axis=0, concat_axis=1, tiled=True)  22.9 us
    unnamed x1, other arithmetic  5.24 us
    unnamed x7, local copies, waits for them, and re-layouts  3.01 us
  transfers between devices with their start and end apart: 3, of which 3 were waited for; matrix products, arithmetic and copies ran while one was open for 0% of the time, Pallas kernels for 0%

commit v1 on v0

v1 whole, which is shorter than its diff:
```python
import functools
import math

import jax
import jax.numpy as jnp
from jax import lax
from jax.experimental import pallas as pl
from jax.experimental.pallas import tpu as pltpu
from jax.sharding import PartitionSpec as P

ITERS = 2

first_coef = 3.4445
second_coef = -4.775
third_coef = 2.0315

ROW_STEP = 16
SEND_COLS = 512


def kernel(
    groups, size, paired,
    counts_ref, grads_hbm, momentum_hbm, update_hbm, new_hbm,
    grads, momentum, fresh, owned, gram_out, gram_in, result, fsdp_sums, grp_sums,
    load_sem, store_sem, own_sem,
    fsdp_send, fsdp_recv, grp_send, grp_recv,
    out_send, out_recv, gram_send, gram_recv, back_send, back_recv,
):
    matrices, rows, width = grads.shape
    half = width // 2
    step_cols = math.gcd(half, SEND_COLS)
    steps = half // step_cols
    f = lax.axis_index("fsdp")
    g = lax.axis_index("grp")

    def dev(a, b):
        return {"fsdp": a, "grp": b}

    if paired:
        core = lax.rem(g, 2)
        base = g - core
        owner_g = base + f // matrices
        owner_m = lax.rem(f, matrices)
        my_half = core
        peer = (f, base + 1 - core)

        def target(m, h):
            return core * matrices + m, base + h
    else:
        owner_g = g
        owner_m = f // 2
        my_half = lax.rem(f, 2)
        peer = (f + 1 - 2 * my_half, g)

        def target(m, h):
            return jnp.int32(2 * m + h), g

    barrier = pltpu.get_barrier_semaphore()
    others = [(lax.rem(f + d, size), g) for d in range(1, size)]
    others += [(f, lax.rem(g + d, groups)) for d in range(1, groups)]
    if paired:
        others += [(lax.rem(f + d, size), base + 1 - core) for d in range(1, size)]
    for a, b in others:
        pl.semaphore_signal(barrier, inc=1, device_id=dev(a, b), device_id_type=pl.DeviceIdType.MESH)

    load_grads = pltpu.make_async_copy(grads_hbm, grads, load_sem.at[0])
    load_momentum = pltpu.make_async_copy(momentum_hbm, momentum, load_sem.at[1])
    load_grads.start()
    load_momentum.start()

    offset = f * rows

    def live_mask(m, r):
        ids = offset + r + lax.broadcasted_iota(jnp.int32, (ROW_STEP, 1), 0)
        return ids < counts_ref[m]

    load_grads.wait()
    acc = jnp.zeros((8, width), jnp.float32)
    for m in range(matrices):
        for r in range(0, rows, ROW_STEP):
            part = jnp.where(live_mask(m, r), grads[m, r:r + ROW_STEP, :].astype(jnp.float32), 0.0)
            part = part * part
            for k in range(0, ROW_STEP, 8):
                acc = acc + part[k:k + 8]
    tile = acc[:, :128]
    for k in range(128, width, 128):
        tile = tile + acc[:, k:k + 128]
    live_rows = jnp.int32(0)
    for m in range(matrices):
        live_rows = live_rows + jnp.clip(counts_ref[m] - offset, 0, rows)
    fsdp_sums[f, 0:8, :] = tile
    fsdp_sums[f, 8:16, :] = jnp.zeros((8, 128), jnp.float32) + live_rows.astype(jnp.float32)

    pl.semaphore_wait(barrier, len(others))

    def exchange(buf, me, count, place, send, recv):
        copies = []
        for d in range(1, count):
            a, b = place(lax.rem(me + d, count))
            copy = pltpu.make_async_remote_copy(
                buf.at[me], buf.at[me], send.at[d], recv.at[d],
                device_id=dev(a, b), device_id_type=pl.DeviceIdType.MESH,
            )
            copy.start()
            copies.append(copy)
        for copy in copies:
            copy.wait_recv()
        total = buf[0]
        for d in range(1, count):
            total = total + buf[d]
        return total, copies

    total, fsdp_copies = exchange(fsdp_sums, f, size, lambda i: (i, g), fsdp_send, fsdp_recv)
    grp_sums[g] = total
    load_momentum.wait()
    total, grp_copies = exchange(grp_sums, g, groups, lambda i: (f, i), grp_send, grp_recv)
    square_sum = jnp.sum(total[0:8], keepdims=True)
    row_total = total[8:9, 0:1]
    clip = jnp.minimum(1.0, lax.rsqrt(square_sum / (row_total * width) + 1e-06))

    def out_copy(m, h):
        a, b = target(m, h)
        copy = pltpu.make_async_remote_copy(
            fresh.at[m, :, pl.ds(h * half, half)],
            owned.at[pl.ds(pl.multiple_of(f * rows, 16), rows), :],
            out_send.at[m * 2 + h], out_recv.at[f],
            device_id=dev(a, b), device_id_type=pl.DeviceIdType.MESH,
        )
        return copy, jnp.logical_and(a == f, b == g)

    for m in range(matrices):
        for h in range(2):
            cols = slice(h * half, (h + 1) * half)
            for r in range(0, rows, ROW_STEP):
                at = (m, slice(r, r + ROW_STEP), cols)
                fresh[at] = jnp.where(
                    live_mask(m, r),
                    0.95 * momentum[at].astype(jnp.float32) + clip * grads[at].astype(jnp.float32),
                    0.0,
                ).astype(jnp.bfloat16)
            copy, mine = out_copy(m, h)

            @pl.when(jnp.logical_not(mine))
            def _():
                copy.start()

            @pl.when(mine)
            def _():
                owned[pl.ds(pl.multiple_of(f * rows, 16), rows), :] = fresh[m, :, cols]

    store_new = pltpu.make_async_copy(fresh, new_hbm, store_sem)
    store_new.start()

    def here(i):
        return jnp.logical_and(i == f, owner_g == g)

    for i in range(size):
        arrive = pltpu.make_async_remote_copy(
            fresh.at[0, :, pl.ds(0, half)], owned.at[pl.ds(i * rows, rows), :],
            out_send.at[0], out_recv.at[i],
            device_id=dev(f, owner_g), device_id_type=pl.DeviceIdType.MESH,
        )

        @pl.when(jnp.logical_not(here(i)))
        def _():
            arrive.wait_recv()

    def dot(a, b):
        return jnp.dot(a.astype(jnp.bfloat16), b.astype(jnp.bfloat16), preferred_element_type=jnp.float32)

    full = owned[...]
    gram = lax.dot_general(full, full, (((1,), (1,)), ((), ())), preferred_element_type=jnp.float32)
    gram_out[...] = gram.astype(jnp.bfloat16)
    gram_copy = pltpu.make_async_remote_copy(
        gram_out, gram_in, gram_send, gram_recv,
        device_id=dev(*peer), device_id_type=pl.DeviceIdType.MESH,
    )
    gram_copy.start()
    gram_copy.wait_recv()
    gram = gram + gram_in[...].astype(jnp.float32)
    order = gram.shape[0]
    diagonal = lax.broadcasted_iota(jnp.int32, (order, order), 0) == lax.broadcasted_iota(
        jnp.int32, (order, order), 1
    )
    trace = jnp.sum(jnp.where(diagonal, gram, 0.0), keepdims=True)
    inverse = 1.0 / (jnp.sqrt(trace) + 1e-07)
    gram = (gram * inverse) * inverse
    poly = second_coef * gram + third_coef * dot(gram, gram)
    mix = poly
    for _ in range(ITERS - 1):
        turned = dot(poly, gram)
        gram = first_coef * first_coef * gram + 2 * first_coef * turned + dot(poly, turned)
        before = poly
        poly = second_coef * gram + third_coef * dot(gram, gram)
        mix = first_coef * (before + poly) + dot(poly, before)
    lead = first_coef ** ITERS
    mix = mix.astype(jnp.bfloat16)
    scale = inverse * (0.2 * math.sqrt(width))

    def back_copy(i, j):
        copy = pltpu.make_async_remote_copy(
            result.at[j, pl.ds(i * rows, rows), :],
            update_hbm.at[
                owner_m, :, pl.ds(pl.multiple_of(my_half * half + j * step_cols, step_cols), step_cols)
            ],
            back_send.at[i * steps + j],
            back_recv.at[(owner_m * 2 + my_half) * steps + j],
            device_id=dev(jnp.int32(i), owner_g), device_id_type=pl.DeviceIdType.MESH,
        )
        local = pltpu.make_async_copy(
            result.at[j, pl.ds(i * rows, rows), :],
            update_hbm.at[
                owner_m, :, pl.ds(pl.multiple_of(my_half * half + j * step_cols, step_cols), step_cols)
            ],
            own_sem.at[j],
        )
        return copy, local

    for j in range(steps):
        block = owned[:, j * step_cols:(j + 1) * step_cols]
        made = lead * block.astype(jnp.float32) + jnp.dot(mix, block, preferred_element_type=jnp.float32)
        result[j] = (scale * made).astype(jnp.bfloat16)
        for i in range(size):
            copy, local = back_copy(i, j)

            @pl.when(jnp.logical_not(here(i)))
            def _():
                copy.start()

            @pl.when(here(i))
            def _():
                local.start()

    for copy in fsdp_copies + grp_copies:
        copy.wait_send()
    gram_copy.wait_send()
    for m in range(matrices):
        for h in range(2):
            copy, mine = out_copy(m, h)

            @pl.when(jnp.logical_not(mine))
            def _():
                copy.wait_send()

    store_new.wait()
    for j in range(steps):
        for i in range(size):
            copy, local = back_copy(i, j)

            @pl.when(jnp.logical_not(here(i)))
            def _():
                copy.wait_send()

            @pl.when(here(i))
            def _():
                local.wait()

    for m in range(matrices):
        for h in range(2):
            a, b = target(m, h)
            for j in range(steps):
                arrive = pltpu.make_async_remote_copy(
                    result.at[j, pl.ds(0, rows), :],
                    update_hbm.at[m, :, pl.ds(h * half + j * step_cols, step_cols)],
                    back_send.at[0], back_recv.at[(m * 2 + h) * steps + j],
                    device_id=dev(a, b), device_id_type=pl.DeviceIdType.MESH,
                )

                @pl.when(jnp.logical_not(jnp.logical_and(a == f, b == g)))
                def _():
                    arrive.wait_recv()


def local(groups, size, paired, grads, momentum, row_counts):
    matrices, rows, width = grads.shape
    half = width // 2
    step_cols = math.gcd(half, SEND_COLS)
    steps = half // step_cols
    order = size * rows
    dma = pltpu.SemaphoreType.DMA
    update, new_momentum = pl.pallas_call(
        functools.partial(kernel, groups, size, paired),
        out_shape=(
            jax.ShapeDtypeStruct(grads.shape, jnp.bfloat16),
            jax.ShapeDtypeStruct(grads.shape, jnp.bfloat16),
        ),
        in_specs=[
            pl.BlockSpec(memory_space=pltpu.SMEM),
            pl.BlockSpec(memory_space=pl.ANY),
            pl.BlockSpec(memory_space=pl.ANY),
        ],
        out_specs=(pl.BlockSpec(memory_space=pl.ANY), pl.BlockSpec(memory_space=pl.ANY)),
        scratch_shapes=[
            pltpu.VMEM(grads.shape, jnp.bfloat16),
            pltpu.VMEM(grads.shape, jnp.bfloat16),
            pltpu.VMEM(grads.shape, jnp.bfloat16),
            pltpu.VMEM((order, half), jnp.bfloat16),
            pltpu.VMEM((order, order), jnp.bfloat16),
            pltpu.VMEM((order, order), jnp.bfloat16),
            pltpu.VMEM((steps, order, step_cols), jnp.bfloat16),
            pltpu.VMEM((size, 16, 128), jnp.float32),
            pltpu.VMEM((groups, 16, 128), jnp.float32),
            dma((2,)),
            dma,
            dma((steps,)),
            dma((size,)),
            dma((size,)),
            dma((groups,)),
            dma((groups,)),
            dma((2 * matrices,)),
            dma((size,)),
            dma,
            dma,
            dma((size * steps,)),
            dma((2 * matrices * steps,)),
        ],
        compiler_params=pltpu.CompilerParams(
            collective_id=0, has_side_effects=True, vmem_limit_bytes=32 * 1024 * 1024
        ),
        cost_estimate=pl.CostEstimate(
            flops=4 * order * order * half, bytes_accessed=8 * grads.size, transcendentals=0
        ),
    )(row_counts, grads, momentum)
    return update, new_momentum


def chips_pair_groups(mesh):
    names = list(mesh.axis_names)
    grid = mesh.devices
    if names != ["fsdp", "grp"] or grid.shape[1] % 2:
        return False
    return all(
        getattr(grid[0, i], "coords", None) is not None
        and tuple(grid[0, i].coords) == tuple(grid[0, i + 1].coords)
        for i in range(0, grid.shape[1], 2)
    )


def solution(mesh):
    placed = (P("grp", "fsdp", None), P("grp", "fsdp", None), P("grp"))
    return jax.shard_map(
        functools.partial(local, mesh.shape["grp"], mesh.shape["fsdp"], chips_pair_groups(mesh)),
        mesh=mesh,
        in_specs=placed,
        out_specs=(P("grp", "fsdp", None), P("grp", "fsdp", None)),
        check_vma=False,
    )
```

time: 148 us -> 55.8 us (0.38)
  the two profiles are of different devices: /device:TPU:0 before, /device:TPU:24 now
where the time goes in v1:
time: 55.8 us; the launch traced here: 55.6 us
  Pallas kernels  50.3 us (90%)
  local copies, waits for them, and re-layouts  4.67 us (8%)
  between operations  0.65 us (1%)
    pallas_call x1, Pallas kernels, local(): pl.pallas_call(functools.partial(kernel, groups, size, paired), out_shape...  50.3 us
    unnamed x8, local copies, waits for them, and re-layouts  4.67 us

profile of v1, /device:TPU:24, one launch (start us, length us, event | category | flops | bytes accessed | tf_op | source)
XLA Modules:
  0.0 55.6 jit_solution(2648950135514620696)
XLA Ops:
  0.6 0.0 copy-start
  0.6 1.1 %copy-done = bf16[2,96,2048]{2,1,0:T(8,128)(2,1)S(1)} copy-done((bf16[2,96,2048]{2,1,0:T(8,128)(2,1)S(1)}, bf16[2,96,2048]{2,1,0:T(8,128)(2,1)}, u32[]{:S(2)}) %copy-start) | copy-done | bytes 786456
  1.8 0.0 copy-start.1
  1.8 1.1 %copy-done.1 = bf16[2,96,2048]{2,1,0:T(8,128)(2,1)S(1)} copy-done((bf16[2,96,2048]{2,1,0:T(8,128)(2,1)S(1)}, bf16[2,96,2048]{2,1,0:T(8,128)(2,1)}, u32[]{:S(2)}) %copy-start.1) | copy-done | bytes 786456
  2.9 0.0 copy-start.2
  2.9 0.7 %copy-done.2 = s32[2]{0:T(128)S(1)} copy-done((s32[2]{0:T(128)S(1)}, s32[2]{0:T(128)}, u32[]{:S(2)}) %copy-start.2) | copy-done | bytes 32
  3.6 50.3 %shard_map.50 = (bf16[2,96,2048]{2,1,0:T(8,128)(2,1)S(1)}, bf16[2,96,2048]{2,1,0:T(8,128)(2,1)S(1)}) custom-call(s32[2]{0:T(128)S(1)} %copy-done.2, bf16[2,96,2048]{2,1,0:T(8,128)(2,1)S(1)} %copy-done, bf16[2,96,2048]{2,1,0:T(8,128)(2,1)S(1)} %copy-done.1), custom_call_target="tpu_custom_call" | custom-call | flops 603979776 | bytes 3145728 | tf_op jit(solution)/shard_map/pallas_call | solution.py:281
  53.8 0.9 %copy.7 = bf16[2,96,2048]{2,1,0:T(8,128)(2,1)} copy(bf16[2,96,2048]{2,1,0:T(8,128)(2,1)S(1)} %get-tuple-element.4) | data formatting | bytes 1572864
  54.7 0.9 %copy.8 = bf16[2,96,2048]{2,1,0:T(8,128)(2,1)} copy(bf16[2,96,2048]{2,1,0:T(8,128)(2,1)S(1)} %get-tuple-element.5) | data formatting | bytes 1572864
Async XLA Ops:
  0.6 1.1 %copy-start = (bf16[2,96,2048]{2,1,0:T(8,128)(2,1)S(1)}, bf16[2,96,2048]{2,1,0:T(8,128)(2,1)}, u32[]{:S(2)}) copy-start(bf16[2,96,2048]{2,1,0:T(8,128)(2,1)} %grads_hbm.1) | copy-start | bytes 2359300
  1.8 1.1 %copy-start.1 = (bf16[2,96,2048]{2,1,0:T(8,128)(2,1)S(1)}, bf16[2,96,2048]{2,1,0:T(8,128)(2,1)}, u32[]{:S(2)}) copy-start(bf16[2,96,2048]{2,1,0:T(8,128)(2,1)} %momentum_hbm.1) | copy-start | bytes 2359300
  2.9 0.7 %copy-start.2 = (s32[2]{0:T(128)S(1)}, s32[2]{0:T(128)}, u32[]{:S(2)}) copy-start(s32[2]{0:T(128)} %counts_ref.1) | copy-start | bytes 28

commit v2 on v1

--- a/solution.py
+++ b/solution.py
@@ -16,13 +16,14 @@
 
 ROW_STEP = 16
 SEND_COLS = 512
+VMEM_BYTES = 63 * 1024 * 1024
 
 
 def kernel(
     groups, size, paired,
-    counts_ref, grads_hbm, momentum_hbm, update_hbm, new_hbm,
-    grads, momentum, fresh, owned, gram_out, gram_in, result, fsdp_sums, grp_sums,
-    load_sem, store_sem, own_sem,
+    counts_hbm, grads_hbm, momentum_hbm, update_hbm, new_hbm,
+    counts_ref, grads, momentum, fresh, owned, gram_out, gram_in, result, fsdp_sums, grp_sums,
+    count_sem, load_sem, store_sem, own_sem,
     fsdp_send, fsdp_recv, grp_send, grp_recv,
     out_send, out_recv, gram_send, gram_recv, back_send, back_recv,
 ):
@@ -63,10 +64,22 @@
     for a, b in others:
         pl.semaphore_signal(barrier, inc=1, device_id=dev(a, b), device_id_type=pl.DeviceIdType.MESH)
 
-    load_grads = pltpu.make_async_copy(grads_hbm, grads, load_sem.at[0])
-    load_momentum = pltpu.make_async_copy(momentum_hbm, momentum, load_sem.at[1])
-    load_grads.start()
-    load_momentum.start()
+    load_counts = pltpu.make_async_copy(counts_hbm, counts_ref, count_sem)
+    load_counts.start()
+    piece = load_rows(rows)
+    loads = [
+        [
+            pltpu.make_async_copy(
+                source.at[m, pl.ds(r, piece), :], kept.at[m, pl.ds(r, piece), :],
+                load_sem.at[k, m * (rows // piece) + r // piece],
+            )
+            for m in range(matrices)
+            for r in range(0, rows, piece)
+        ]
+        for k, (source, kept) in enumerate(((grads_hbm, grads), (momentum_hbm, momentum)))
+    ]
+    for load in loads[0] + loads[1]:
+        load.start()
 
     offset = f * rows
 
@@ -74,10 +87,12 @@
         ids = offset + r + lax.broadcasted_iota(jnp.int32, (ROW_STEP, 1), 0)
         return ids < counts_ref[m]
 
-    load_grads.wait()
+    load_counts.wait()
     acc = jnp.zeros((8, width), jnp.float32)
     for m in range(matrices):
         for r in range(0, rows, ROW_STEP):
+            if r % piece == 0:
+                loads[0][m * (rows // piece) + r // piece].wait()
             part = jnp.where(live_mask(m, r), grads[m, r:r + ROW_STEP, :].astype(jnp.float32), 0.0)
             part = part * part
             for k in range(0, ROW_STEP, 8):
@@ -112,7 +127,8 @@
 
     total, fsdp_copies = exchange(fsdp_sums, f, size, lambda i: (i, g), fsdp_send, fsdp_recv)
     grp_sums[g] = total
-    load_momentum.wait()
+    for load in loads[1]:
+        load.wait()
     total, grp_copies = exchange(grp_sums, g, groups, lambda i: (f, i), grp_send, grp_recv)
     square_sum = jnp.sum(total[0:8], keepdims=True)
     row_total = total[8:9, 0:1]
@@ -271,6 +287,22 @@
                     arrive.wait_recv()
 
 
+def load_rows(rows):
+    return 32 if rows % 32 == 0 else rows
+
+
+def store(update, new, update_hbm, new_hbm, sems):
+    copies = [
+        pltpu.make_async_copy(source.at[m], kept.at[m], sems.at[k, m])
+        for k, (source, kept) in enumerate(((update, update_hbm), (new, new_hbm)))
+        for m in range(update.shape[0])
+    ]
+    for copy in copies:
+        copy.start()
+    for copy in copies:
+        copy.wait()
+
+
 def local(groups, size, paired, grads, momentum, row_counts):
     matrices, rows, width = grads.shape
     half = width // 2
@@ -285,12 +317,13 @@
             jax.ShapeDtypeStruct(grads.shape, jnp.bfloat16),
         ),
         in_specs=[
-            pl.BlockSpec(memory_space=pltpu.SMEM),
-            pl.BlockSpec(memory_space=pl.ANY),
-            pl.BlockSpec(memory_space=pl.ANY),
+            pl.BlockSpec(memory_space=pltpu.HBM),
+            pl.BlockSpec(memory_space=pltpu.HBM),
+            pl.BlockSpec(memory_space=pltpu.HBM),
         ],
         out_specs=(pl.BlockSpec(memory_space=pl.ANY), pl.BlockSpec(memory_space=pl.ANY)),
         scratch_shapes=[
+            pltpu.SMEM(row_counts.shape, jnp.int32),
             pltpu.VMEM(grads.shape, jnp.bfloat16),
             pltpu.VMEM(grads.shape, jnp.bfloat16),
             pltpu.VMEM(grads.shape, jnp.bfloat16),
@@ -300,7 +333,8 @@
             pltpu.VMEM((steps, order, step_cols), jnp.bfloat16),
             pltpu.VMEM((size, 16, 128), jnp.float32),
             pltpu.VMEM((groups, 16, 128), jnp.float32),
-            dma((2,)),
+            dma,
+            dma((2, matrices * (rows // load_rows(rows)))),
             dma,
             dma((steps,)),
             dma((size,)),
@@ -315,13 +349,23 @@
             dma((2 * matrices * steps,)),
         ],
         compiler_params=pltpu.CompilerParams(
-            collective_id=0, has_side_effects=True, vmem_limit_bytes=32 * 1024 * 1024
+            collective_id=0, has_side_effects=True, vmem_limit_bytes=VMEM_BYTES
         ),
         cost_estimate=pl.CostEstimate(
             flops=4 * order * order * half, bytes_accessed=8 * grads.size, transcendentals=0
         ),
     )(row_counts, grads, momentum)
-    return update, new_momentum
+    return pl.pallas_call(
+        store,
+        out_shape=(
+            jax.ShapeDtypeStruct(grads.shape, jnp.bfloat16),
+            jax.ShapeDtypeStruct(grads.shape, jnp.bfloat16),
+        ),
+        in_specs=[pl.BlockSpec(memory_space=pl.ANY)] * 2,
+        out_specs=(pl.BlockSpec(memory_space=pltpu.HBM), pl.BlockSpec(memory_space=pltpu.HBM)),
+        scratch_shapes=[dma((2, matrices))],
+        compiler_params=pltpu.CompilerParams(vmem_limit_bytes=VMEM_BYTES),
+    )(update, new_momentum)
 
 
 def chips_pair_groups(mesh):

time: 55.8 us -> 99.5 us (1.78)
  Pallas kernels: 50.3 us -> 98.7 us
  local copies, waits for them, and re-layouts: 4.67 us -> 0 us
    pallas_call x0 -> x1, Pallas kernels: none -> 48.8 us  [local(): pl.pallas_call(store, out_shape=(jax.ShapeDtypeStruct(grads.shape, jnp.bf...]
    unnamed x8 -> x0, local copies, waits for them, and re-layouts: 4.67 us -> none
where the time goes in v2:
time: 99.5 us; the launch traced here: 99.4 us
  Pallas kernels  98.7 us (99%)
    pallas_call x1, Pallas kernels, local(): pl.pallas_call(functools.partial(kernel, groups, size, paired), out_shape...  49.9 us
    pallas_call x1, Pallas kernels, local(): pl.pallas_call(store, out_shape=(jax.ShapeDtypeStruct(grads.shape, jnp.bf...  48.8 us

profile of v2, /device:TPU:24, one launch (start us, length us, event | category | flops | bytes accessed | tf_op | source)
XLA Modules:
  0.0 99.4 jit_solution(4417754632670219730)
XLA Ops:
  0.6 49.9 %shard_map.50 = (bf16[2,96,2048]{2,1,0:T(8,128)(2,1)}, bf16[2,96,2048]{2,1,0:T(8,128)(2,1)}) custom-call(s32[2]{0:T(128)} %counts_hbm.1, bf16[2,96,2048]{2,1,0:T(8,128)(2,1)} %grads_hbm.1, bf16[2,96,2048]{2,1,0:T(8,128)(2,1)} %momentum_hbm.1), custom_call_target="tpu_custom_call" | custom-call | flops 603979776 | bytes 3145728 | tf_op jit(solution)/shard_map/pallas_call | solution.py:313
  50.6 48.8 %shard_map.51 = (bf16[2,96,2048]{2,1,0:T(8,128)(2,1)}, bf16[2,96,2048]{2,1,0:T(8,128)(2,1)}) custom-call(bf16[2,96,2048]{2,1,0:T(8,128)(2,1)} %get-tuple-element.4.update, bf16[2,96,2048]{2,1,0:T(8,128)(2,1)} %get-tuple-element.5.new), custom_call_target="tpu_custom_call" | custom-call | tf_op jit(solution)/shard_map/pallas_call | solution.py:358

commit v3 on v2

--- a/solution.py
+++ b/solution.py
@@ -289,18 +289,6 @@
 
 def load_rows(rows):
     return 32 if rows % 32 == 0 else rows
-
-
-def store(update, new, update_hbm, new_hbm, sems):
-    copies = [
-        pltpu.make_async_copy(source.at[m], kept.at[m], sems.at[k, m])
-        for k, (source, kept) in enumerate(((update, update_hbm), (new, new_hbm)))
-        for m in range(update.shape[0])
-    ]
-    for copy in copies:
-        copy.start()
-    for copy in copies:
-        copy.wait()
 
 
 def local(groups, size, paired, grads, momentum, row_counts):
@@ -355,17 +343,7 @@
             flops=4 * order * order * half, bytes_accessed=8 * grads.size, transcendentals=0
         ),
     )(row_counts, grads, momentum)
-    return pl.pallas_call(
-        store,
-        out_shape=(
-            jax.ShapeDtypeStruct(grads.shape, jnp.bfloat16),
-            jax.ShapeDtypeStruct(grads.shape, jnp.bfloat16),
-        ),
-        in_specs=[pl.BlockSpec(memory_space=pl.ANY)] * 2,
-        out_specs=(pl.BlockSpec(memory_space=pltpu.HBM), pl.BlockSpec(memory_space=pltpu.HBM)),
-        scratch_shapes=[dma((2, matrices))],
-        compiler_params=pltpu.CompilerParams(vmem_limit_bytes=VMEM_BYTES),
-    )(update, new_momentum)
+    return update, new_momentum
 
 
 def chips_pair_groups(mesh):

time: 99.5 us -> 53.8 us (0.54)
  Pallas kernels: 98.7 us -> 49.9 us
  local copies, waits for them, and re-layouts: 0 us -> 3.04 us
    pallas_call x1 -> x0, Pallas kernels: 48.8 us -> none  [local(): pl.pallas_call(store, out_shape=(jax.ShapeDtypeStruct(grads.shape, jnp.bf...]
    unnamed x0 -> x4, local copies, waits for them, and re-layouts: none -> 3.04 us
where the time goes in v3:
time: 53.8 us; the launch traced here: 53.6 us
  Pallas kernels  49.9 us (93%)
  local copies, waits for them, and re-layouts  3.04 us (6%)
  between operations  0.65 us (1%)
    pallas_call x1, Pallas kernels, local(): pl.pallas_call(functools.partial(kernel, groups, size, paired), out_shape...  49.9 us
    unnamed x4, local copies, waits for them, and re-layouts  3.04 us

profile of v3, /device:TPU:24, one launch (start us, length us, event | category | flops | bytes accessed | tf_op | source)
XLA Modules:
  0.0 53.6 jit_solution(9593442951210215105)
XLA Ops:
  0.6 49.9 %shard_map.50 = (bf16[2,96,2048]{2,1,0:T(8,128)(2,1)}, bf16[2,96,2048]{2,1,0:T(8,128)(2,1)}) custom-call(s32[2]{0:T(128)} %counts_hbm.1, bf16[2,96,2048]{2,1,0:T(8,128)(2,1)} %grads_hbm.1, bf16[2,96,2048]{2,1,0:T(8,128)(2,1)} %momentum_hbm.1), custom_call_target="tpu_custom_call" | custom-call | flops 603979776 | bytes 3145728 | tf_op jit(solution)/shard_map/pallas_call | solution.py:301
  50.6 0.0 copy-start
  50.6 2.2 %copy.7 = bf16[2,96,2048]{2,1,0:T(8,128)(2,1)} copy(bf16[2,96,2048]{2,1,0:T(8,128)(2,1)} %get-tuple-element.4) | data formatting | bytes 1572864
  52.8 0.0 copy-done
  52.8 0.9 %copy.8 = bf16[2,96,2048]{2,1,0:T(8,128)(2,1)} copy(bf16[2,96,2048]{2,1,0:T(8,128)(2,1)S(1)} %copy-done) | data formatting | bytes 1572864
Async XLA Ops:
  50.6 2.2 %copy-start = (bf16[2,96,2048]{2,1,0:T(8,128)(2,1)S(1)}, bf16[2,96,2048]{2,1,0:T(8,128)(2,1)}, u32[]{:S(2)}) copy-start(bf16[2,96,2048]{2,1,0:T(8,128)(2,1)} %get-tuple-element.5) | copy-start | bytes 2359300

commit v4 on v3

--- a/solution.py
+++ b/solution.py
@@ -47,6 +47,9 @@
 
         def target(m, h):
             return core * matrices + m, base + h
+
+        def nth(k):
+            return jnp.where(core == 1, k, matrices - 1 - k)
     else:
         owner_g = g
         owner_m = f // 2
@@ -55,6 +58,9 @@
 
         def target(m, h):
             return jnp.int32(2 * m + h), g
+
+        def nth(k):
+            return k
 
     barrier = pltpu.get_barrier_semaphore()
     others = [(lax.rem(f + d, size), g) for d in range(1, size)]
@@ -134,17 +140,27 @@
     row_total = total[8:9, 0:1]
     clip = jnp.minimum(1.0, lax.rsqrt(square_sum / (row_total * width) + 1e-06))
 
-    def out_copy(m, h):
+    def out_copy(k, h):
+        m = nth(k)
         a, b = target(m, h)
         copy = pltpu.make_async_remote_copy(
             fresh.at[m, :, pl.ds(h * half, half)],
             owned.at[pl.ds(pl.multiple_of(f * rows, 16), rows), :],
-            out_send.at[m * 2 + h], out_recv.at[f],
+            out_send.at[k * 2 + h], out_recv.at[f],
             device_id=dev(a, b), device_id_type=pl.DeviceIdType.MESH,
         )
         return copy, jnp.logical_and(a == f, b == g)
 
-    for m in range(matrices):
+    def wait_out(k):
+        for h in range(2):
+            copy, mine = out_copy(k, h)
+
+            @pl.when(jnp.logical_not(mine))
+            def _():
+                copy.wait_send()
+
+    for k in range(matrices):
+        m = nth(k)
         for h in range(2):
             cols = slice(h * half, (h + 1) * half)
             for r in range(0, rows, ROW_STEP):
@@ -154,7 +170,10 @@
                     0.95 * momentum[at].astype(jnp.float32) + clip * grads[at].astype(jnp.float32),
                     0.0,
                 ).astype(jnp.bfloat16)
-            copy, mine = out_copy(m, h)
+        if k:
+            wait_out(k - 1)
+        for h in range(2):
+            copy, mine = out_copy(k, h)
 
             @pl.when(jnp.logical_not(mine))
             def _():
@@ -162,6 +181,7 @@
 
             @pl.when(mine)
             def _():
+                cols = slice(h * half, (h + 1) * half)
                 owned[pl.ds(pl.multiple_of(f * rows, 16), rows), :] = fresh[m, :, cols]
 
     store_new = pltpu.make_async_copy(fresh, new_hbm, store_sem)
@@ -213,18 +233,22 @@
     mix = mix.astype(jnp.bfloat16)
     scale = inverse * (0.2 * math.sqrt(width))
 
-    def back_copy(i, j):
+    def back_to(d):
+        return jnp.where(f < size // 2, size - 1 - d, d)
+
+    def back_copy(d, j):
+        i = back_to(d)
         copy = pltpu.make_async_remote_copy(
-            result.at[j, pl.ds(i * rows, rows), :],
+            result.at[j, pl.ds(pl.multiple_of(i * rows, 16), rows), :],
             update_hbm.at[
                 owner_m, :, pl.ds(pl.multiple_of(my_half * half + j * step_cols, step_cols), step_cols)
             ],
-            back_send.at[i * steps + j],
+            back_send.at[d * steps + j],
             back_recv.at[(owner_m * 2 + my_half) * steps + j],
-            device_id=dev(jnp.int32(i), owner_g), device_id_type=pl.DeviceIdType.MESH,
+            device_id=dev(i, owner_g), device_id_type=pl.DeviceIdType.MESH,
         )
         local = pltpu.make_async_copy(
-            result.at[j, pl.ds(i * rows, rows), :],
+            result.at[j, pl.ds(pl.multiple_of(i * rows, 16), rows), :],
             update_hbm.at[
                 owner_m, :, pl.ds(pl.multiple_of(my_half * half + j * step_cols, step_cols), step_cols)
             ],
@@ -236,38 +260,31 @@
         block = owned[:, j * step_cols:(j + 1) * step_cols]
         made = lead * block.astype(jnp.float32) + jnp.dot(mix, block, preferred_element_type=jnp.float32)
         result[j] = (scale * made).astype(jnp.bfloat16)
-        for i in range(size):
-            copy, local = back_copy(i, j)
-
-            @pl.when(jnp.logical_not(here(i)))
+        for d in range(size):
+            copy, local = back_copy(d, j)
+
+            @pl.when(jnp.logical_not(here(back_to(d))))
             def _():
                 copy.start()
 
-            @pl.when(here(i))
+            @pl.when(here(back_to(d)))
             def _():
                 local.start()
 
     for copy in fsdp_copies + grp_copies:
         copy.wait_send()
     gram_copy.wait_send()
-    for m in range(matrices):
-        for h in range(2):
-            copy, mine = out_copy(m, h)
-
-            @pl.when(jnp.logical_not(mine))
-            def _():
-                copy.wait_send()
-
+    wait_out(matrices - 1)
     store_new.wait()
     for j in range(steps):
-        for i in range(size):
-            copy, local = back_copy(i, j)
-
-            @pl.when(jnp.logical_not(here(i)))
+        for d in range(size):
+            copy, local = back_copy(d, j)
+
+            @pl.when(jnp.logical_not(here(back_to(d))))
             def _():
                 copy.wait_send()
 
-            @pl.when(here(i))
+            @pl.when(here(back_to(d)))
             def _():
                 local.wait()
 

time: 53.8 us -> 55.8 us (1.037)
  the two profiles are of different devices: /device:TPU:24 before, /device:TPU:0 now
where the time goes in v4:
time: 55.8 us; the launch traced here: 55.7 us
  Pallas kernels  52 us (93%)
  local copies, waits for them, and re-layouts  3.04 us (5%)
  between operations  0.65 us (1%)
    pallas_call x1, Pallas kernels, local(): pl.pallas_call(functools.partial(kernel, groups, size, paired), out_shape...  52 us
    unnamed x4, local copies, waits for them, and re-layouts  3.04 us

profile of v4, /device:TPU:0, one launch (start us, length us, event | category | flops | bytes accessed | tf_op | source)
XLA Modules:
  0.0 55.7 jit_solution(11979376364755660387)
XLA Ops:
  0.6 52.0 %shard_map.50 = (bf16[2,96,2048]{2,1,0:T(8,128)(2,1)}, bf16[2,96,2048]{2,1,0:T(8,128)(2,1)}) custom-call(s32[2]{0:T(128)} %counts_hbm.1, bf16[2,96,2048]{2,1,0:T(8,128)(2,1)} %grads_hbm.1, bf16[2,96,2048]{2,1,0:T(8,128)(2,1)} %momentum_hbm.1), custom_call_target="tpu_custom_call" | custom-call | flops 603979776 | bytes 3145728 | tf_op jit(solution)/shard_map/pallas_call | solution.py:318
  52.6 0.0 copy-start
  52.6 2.2 %copy.7 = bf16[2,96,2048]{2,1,0:T(8,128)(2,1)} copy(bf16[2,96,2048]{2,1,0:T(8,128)(2,1)} %get-tuple-element.4) | data formatting | bytes 1572864
  54.8 0.0 copy-done
  54.8 0.9 %copy.8 = bf16[2,96,2048]{2,1,0:T(8,128)(2,1)} copy(bf16[2,96,2048]{2,1,0:T(8,128)(2,1)S(1)} %copy-done) | data formatting | bytes 1572864
Async XLA Ops:
  52.6 2.2 %copy-start = (bf16[2,96,2048]{2,1,0:T(8,128)(2,1)S(1)}, bf16[2,96,2048]{2,1,0:T(8,128)(2,1)}, u32[]{:S(2)}) copy-start(bf16[2,96,2048]{2,1,0:T(8,128)(2,1)} %get-tuple-element.5) | copy-start | bytes 2359300

commit v5 on v2

--- a/solution.py
+++ b/solution.py
@@ -16,7 +16,7 @@
 
 ROW_STEP = 16
 SEND_COLS = 512
-VMEM_BYTES = 63 * 1024 * 1024
+VMEM_BYTES = 40 * 1024 * 1024
 
 
 def kernel(
@@ -310,6 +310,9 @@
     steps = half // step_cols
     order = size * rows
     dma = pltpu.SemaphoreType.DMA
+    grads, momentum, row_counts = (
+        pltpu.with_memory_space_constraint(value, pltpu.HBM) for value in (grads, momentum, row_counts)
+    )
     update, new_momentum = pl.pallas_call(
         functools.partial(kernel, groups, size, paired),
         out_shape=(

time: 99.5 us -> 51.8 us (0.52)
  Pallas kernels: 98.7 us -> 51 us
    pallas_call x1, Pallas kernels: 48.8 us -> 1.17 us  [local(): pl.pallas_call(store, out_shape=(jax.ShapeDtypeStruct(grads.shape, jnp.bf...]
where the time goes in v5:
time: 51.8 us; the launch traced here: 51.7 us
  Pallas kernels  51 us (98%)
  between operations  0.64 us (1%)
    pallas_call x1, Pallas kernels, local(): pl.pallas_call(functools.partial(kernel, groups, size, paired), out_shape...  49.8 us
    pallas_call x1, Pallas kernels, local(): pl.pallas_call(store, out_shape=(jax.ShapeDtypeStruct(grads.shape, jnp.bf...  1.17 us

profile of v5, /device:TPU:24, one launch (start us, length us, event | category | flops | bytes accessed | tf_op | source)
XLA Modules:
  0.0 51.7 jit_solution(3655747168967889031)
XLA Ops:
  0.6 49.8 %shard_map.50 = (bf16[2,96,2048]{2,1,0:T(8,128)(2,1)S(1)}, bf16[2,96,2048]{2,1,0:T(8,128)(2,1)S(1)}) custom-call(s32[2]{0:T(128)} %counts_hbm.1, bf16[2,96,2048]{2,1,0:T(8,128)(2,1)} %grads_hbm.1, bf16[2,96,2048]{2,1,0:T(8,128)(2,1)} %momentum_hbm.1), custom_call_target="tpu_custom_call" | custom-call | flops 603979776 | bytes 3145728 | tf_op jit(solution)/shard_map/pallas_call | solution.py:316
  50.5 1.2 %shard_map.51 = (bf16[2,96,2048]{2,1,0:T(8,128)(2,1)}, bf16[2,96,2048]{2,1,0:T(8,128)(2,1)}) custom-call(bf16[2,96,2048]{2,1,0:T(8,128)(2,1)S(1)} %get-tuple-element.4.update, bf16[2,96,2048]{2,1,0:T(8,128)(2,1)S(1)} %get-tuple-element.5.new), custom_call_target="tpu_custom_call" | custom-call | tf_op jit(solution)/shard_map/pallas_call | solution.py:361

commit v6 on v5

--- a/solution.py
+++ b/solution.py
@@ -16,16 +16,17 @@
 
 ROW_STEP = 16
 SEND_COLS = 512
+RAW_COLS = 128
 VMEM_BYTES = 40 * 1024 * 1024
 
 
 def kernel(
     groups, size, paired,
     counts_hbm, grads_hbm, momentum_hbm, update_hbm, new_hbm,
-    counts_ref, grads, momentum, fresh, owned, gram_out, gram_in, result, fsdp_sums, grp_sums,
+    counts_ref, grads, momentum, fresh, owned, raw_out, raw_in, gram_out, gram_in, result, fsdp_sums, grp_sums,
     count_sem, load_sem, store_sem, own_sem,
     fsdp_send, fsdp_recv, grp_send, grp_recv,
-    out_send, out_recv, gram_send, gram_recv, back_send, back_recv,
+    raw_send, raw_recv, out_send, out_recv, gram_send, gram_recv, back_send, back_recv,
 ):
     matrices, rows, width = grads.shape
     half = width // 2
@@ -118,18 +119,45 @@
             )
             copy.start()
             copies.append(copy)
+        return copies
+
+    def added(buf, copies):
         for copy in copies:
             copy.wait_recv()
         total = buf[0]
-        for d in range(1, count):
+        for d in range(1, buf.shape[0]):
             total = total + buf[d]
-        return total, copies
-
-    total, fsdp_copies = exchange(fsdp_sums, f, size, lambda i: (i, g), fsdp_send, fsdp_recv)
-    grp_sums[g] = total
+        return total
+
+    def raw_copy(m, h):
+        a, b = target(m, h)
+        copy = pltpu.make_async_remote_copy(
+            raw_out.at[m, h],
+            raw_in.at[:, pl.ds(pl.multiple_of(f * rows, 16), rows), :],
+            raw_send.at[m * 2 + h], raw_recv.at[f],
+            device_id=dev(a, b), device_id_type=pl.DeviceIdType.MESH,
+        )
+        return copy, jnp.logical_and(a == f, b == g)
+
+    fsdp_copies = exchange(fsdp_sums, f, size, lambda i: (i, g), fsdp_send, fsdp_recv)
     for load in loads[1]:
         load.wait()
-    total, grp_copies = exchange(grp_sums, g, groups, lambda i: (f, i), grp_send, grp_recv)
+    for m in range(matrices):
+        for h in range(2):
+            for r in range(0, rows, ROW_STEP):
+                live = live_mask(m, r)
+                for k, kept in enumerate((grads, momentum)):
+                    value = kept[m, r:r + ROW_STEP, h * half:h * half + RAW_COLS].astype(jnp.float32)
+                    raw_out[m, h, k, r:r + ROW_STEP, :] = jnp.where(live, value, 0.0).astype(jnp.bfloat16)
+            copy, mine = raw_copy(m, h)
+
+            @pl.when(jnp.logical_not(mine))
+            def _():
+                copy.start()
+
+    grp_sums[g] = added(fsdp_sums, fsdp_copies)
+    grp_copies = exchange(grp_sums, g, groups, lambda i: (f, i), grp_send, grp_recv)
+    total = added(grp_sums, grp_copies)
     square_sum = jnp.sum(total[0:8], keepdims=True)
     row_total = total[8:9, 0:1]
     clip = jnp.minimum(1.0, lax.rsqrt(square_sum / (row_total * width) + 1e-06))
@@ -137,8 +165,8 @@
     def out_copy(m, h):
         a, b = target(m, h)
         copy = pltpu.make_async_remote_copy(
-            fresh.at[m, :, pl.ds(h * half, half)],
-            owned.at[pl.ds(pl.multiple_of(f * rows, 16), rows), :],
+            fresh.at[m, :, pl.ds(h * half + RAW_COLS, half - RAW_COLS)],
+            owned.at[pl.ds(pl.multiple_of(f * rows, 16), rows), pl.ds(RAW_COLS, half - RAW_COLS)],
             out_send.at[m * 2 + h], out_recv.at[f],
             device_id=dev(a, b), device_id_type=pl.DeviceIdType.MESH,
         )
@@ -171,8 +199,25 @@
         return jnp.logical_and(i == f, owner_g == g)
 
     for i in range(size):
+        raw_arrive = pltpu.make_async_remote_copy(
+            raw_out.at[0, 0], raw_in.at[:, pl.ds(i * rows, rows), :],
+            raw_send.at[0], raw_recv.at[i],
+            device_id=dev(f, owner_g), device_id_type=pl.DeviceIdType.MESH,
+        )
+
+        @pl.when(jnp.logical_not(here(i)))
+        def _():
+            raw_arrive.wait_recv()
+            for r in range(i * rows, (i + 1) * rows, ROW_STEP):
+                owned[r:r + ROW_STEP, 0:RAW_COLS] = (
+                    0.95 * raw_in[1, r:r + ROW_STEP, :].astype(jnp.float32)
+                    + clip * raw_in[0, r:r + ROW_STEP, :].astype(jnp.float32)
+                ).astype(jnp.bfloat16)
+
+    for i in range(size):
         arrive = pltpu.make_async_remote_copy(
-            fresh.at[0, :, pl.ds(0, half)], owned.at[pl.ds(i * rows, rows), :],
+            fresh.at[0, :, pl.ds(RAW_COLS, half - RAW_COLS)],
+            owned.at[pl.ds(i * rows, rows), pl.ds(RAW_COLS, half - RAW_COLS)],
             out_send.at[0], out_recv.at[i],
             device_id=dev(f, owner_g), device_id_type=pl.DeviceIdType.MESH,
         )
@@ -253,9 +298,11 @@
     for m in range(matrices):
         for h in range(2):
             copy, mine = out_copy(m, h)
+            raw, _ = raw_copy(m, h)
 
             @pl.when(jnp.logical_not(mine))
             def _():
+                raw.wait_send()
                 copy.wait_send()
 
     store_new.wait()
@@ -331,6 +378,8 @@
             pltpu.VMEM(grads.shape, jnp.bfloat16),
             pltpu.VMEM(grads.shape, jnp.bfloat16),
             pltpu.VMEM((order, half), jnp.bfloat16),
+            pltpu.VMEM((matrices, 2, 2, rows, RAW_COLS), jnp.bfloat16),
+            pltpu.VMEM((2, order, RAW_COLS), jnp.bfloat16),
             pltpu.VMEM((order, order), jnp.bfloat16),
             pltpu.VMEM((order, order), jnp.bfloat16),
             pltpu.VMEM((steps, order, step_cols), jnp.bfloat16),
@@ -344,6 +393,8 @@
             dma((size,)),
             dma((groups,)),
             dma((groups,)),
+            dma((2 * matrices,)),
+            dma((size,)),
             dma((2 * matrices,)),
             dma((size,)),
             dma,

time: 51.8 us -> 50.4 us (0.973)
  Pallas kernels: 51 us -> 49.6 us
    pallas_call x1, Pallas kernels: 49.8 us -> 48.4 us  [local(): pl.pallas_call(functools.partial(kernel, groups, size, paired), out_shape...]
where the time goes in v6:
time: 50.4 us; the launch traced here: 50.2 us
  Pallas kernels  49.6 us (98%)
  between operations  0.64 us (1%)
    pallas_call x1, Pallas kernels, local(): pl.pallas_call(functools.partial(kernel, groups, size, paired), out_shape...  48.4 us
    pallas_call x1, Pallas kernels, local(): pl.pallas_call(store, out_shape=(jax.ShapeDtypeStruct(grads.shape, jnp.bf...  1.17 us

profile of v6, /device:TPU:24, one launch (start us, length us, event | category | flops | bytes accessed | tf_op | source)
XLA Modules:
  0.0 50.2 jit_solution(7052231254572463752)
XLA Ops:
  0.6 48.4 %shard_map.50 = (bf16[2,96,2048]{2,1,0:T(8,128)(2,1)S(1)}, bf16[2,96,2048]{2,1,0:T(8,128)(2,1)S(1)}) custom-call(s32[2]{0:T(128)} %counts_hbm.1, bf16[2,96,2048]{2,1,0:T(8,128)(2,1)} %grads_hbm.1, bf16[2,96,2048]{2,1,0:T(8,128)(2,1)} %momentum_hbm.1), custom_call_target="tpu_custom_call" | custom-call | flops 603979776 | bytes 3145728 | tf_op jit(solution)/shard_map/pallas_call | solution.py:363
  49.0 1.2 %shard_map.51 = (bf16[2,96,2048]{2,1,0:T(8,128)(2,1)}, bf16[2,96,2048]{2,1,0:T(8,128)(2,1)}) custom-call(bf16[2,96,2048]{2,1,0:T(8,128)(2,1)S(1)} %get-tuple-element.4.update, bf16[2,96,2048]{2,1,0:T(8,128)(2,1)S(1)} %get-tuple-element.5.new), custom_call_target="tpu_custom_call" | custom-call | tf_op jit(solution)/shard_map/pallas_call | solution.py:412

commit v7 on v6

--- a/solution.py
+++ b/solution.py
@@ -8,14 +8,12 @@
 from jax.experimental.pallas import tpu as pltpu
 from jax.sharding import PartitionSpec as P
 
-ITERS = 2
-
 first_coef = 3.4445
 second_coef = -4.775
 third_coef = 2.0315
 
 ROW_STEP = 16
-SEND_COLS = 512
+SEND_COLS = 256
 RAW_COLS = 128
 VMEM_BYTES = 40 * 1024 * 1024
 
@@ -48,6 +46,9 @@
 
         def target(m, h):
             return core * matrices + m, base + h
+
+        def nth(k):
+            return jnp.where(core == 1, matrices - 1 - k, k)
     else:
         owner_g = g
         owner_m = f // 2
@@ -56,6 +57,9 @@
 
         def target(m, h):
             return jnp.int32(2 * m + h), g
+
+        def nth(k):
+            return k
 
     barrier = pltpu.get_barrier_semaphore()
     others = [(lax.rem(f + d, size), g) for d in range(1, size)]
@@ -162,17 +166,19 @@
     row_total = total[8:9, 0:1]
     clip = jnp.minimum(1.0, lax.rsqrt(square_sum / (row_total * width) + 1e-06))
 
-    def out_copy(m, h):
+    def out_copy(k, h):
+        m = nth(k)
         a, b = target(m, h)
         copy = pltpu.make_async_remote_copy(
             fresh.at[m, :, pl.ds(h * half + RAW_COLS, half - RAW_COLS)],
             owned.at[pl.ds(pl.multiple_of(f * rows, 16), rows), pl.ds(RAW_COLS, half - RAW_COLS)],
-            out_send.at[m * 2 + h], out_recv.at[f],
+            out_send.at[k * 2 + h], out_recv.at[f],
             device_id=dev(a, b), device_id_type=pl.DeviceIdType.MESH,
         )
         return copy, jnp.logical_and(a == f, b == g)
 
-    for m in range(matrices):
+    for k in range(matrices):
+        m = nth(k)
         for h in range(2):
             cols = slice(h * half, (h + 1) * half)
             for r in range(0, rows, ROW_STEP):
@@ -182,7 +188,7 @@
                     0.95 * momentum[at].astype(jnp.float32) + clip * grads[at].astype(jnp.float32),
                     0.0,
                 ).astype(jnp.bfloat16)
-            copy, mine = out_copy(m, h)
+            copy, mine = out_copy(k, h)
 
             @pl.when(jnp.logical_not(mine))
             def _():
@@ -247,29 +253,33 @@
     inverse = 1.0 / (jnp.sqrt(trace) + 1e-07)
     gram = (gram * inverse) * inverse
     poly = second_coef * gram + third_coef * dot(gram, gram)
-    mix = poly
-    for _ in range(ITERS - 1):
-        turned = dot(poly, gram)
-        gram = first_coef * first_coef * gram + 2 * first_coef * turned + dot(poly, turned)
-        before = poly
-        poly = second_coef * gram + third_coef * dot(gram, gram)
-        mix = first_coef * (before + poly) + dot(poly, before)
-    lead = first_coef ** ITERS
+    both = dot(poly, jnp.concatenate([gram.astype(jnp.bfloat16), poly.astype(jnp.bfloat16)], axis=1))
+    turned = first_coef * gram + both[:, :order]
+    rest = 2 * first_coef * poly + both[:, order:]
+    both = dot(turned, jnp.concatenate([poly.astype(jnp.bfloat16), rest.astype(jnp.bfloat16)], axis=1))
+    after = first_coef * turned + both[:, :order]
+    carried = first_coef * first_coef * turned + both[:, order:]
+    mix = first_coef * poly + second_coef * carried + third_coef * dot(after, carried)
+    lead = first_coef * first_coef
     mix = mix.astype(jnp.bfloat16)
     scale = inverse * (0.2 * math.sqrt(width))
 
-    def back_copy(i, j):
+    def back_to(d):
+        return jnp.where(f < size // 2, size - 1 - d, d)
+
+    def back_copy(d, j):
+        i = back_to(d)
         copy = pltpu.make_async_remote_copy(
-            result.at[j, pl.ds(i * rows, rows), :],
+            result.at[j, pl.ds(pl.multiple_of(i * rows, 16), rows), :],
             update_hbm.at[
                 owner_m, :, pl.ds(pl.multiple_of(my_half * half + j * step_cols, step_cols), step_cols)
             ],
-            back_send.at[i * steps + j],
+            back_send.at[d * steps + j],
             back_recv.at[(owner_m * 2 + my_half) * steps + j],
-            device_id=dev(jnp.int32(i), owner_g), device_id_type=pl.DeviceIdType.MESH,
+            device_id=dev(i, owner_g), device_id_type=pl.DeviceIdType.MESH,
         )
         local = pltpu.make_async_copy(
-            result.at[j, pl.ds(i * rows, rows), :],
+            result.at[j, pl.ds(pl.multiple_of(i * rows, 16), rows), :],
             update_hbm.at[
                 owner_m, :, pl.ds(pl.multiple_of(my_half * half + j * step_cols, step_cols), step_cols)
             ],
@@ -281,40 +291,43 @@
         block = owned[:, j * step_cols:(j + 1) * step_cols]
         made = lead * block.astype(jnp.float32) + jnp.dot(mix, block, preferred_element_type=jnp.float32)
         result[j] = (scale * made).astype(jnp.bfloat16)
-        for i in range(size):
-            copy, local = back_copy(i, j)
-
-            @pl.when(jnp.logical_not(here(i)))
+        for d in range(size):
+            copy, local = back_copy(d, j)
+
+            @pl.when(jnp.logical_not(here(back_to(d))))
             def _():
                 copy.start()
 
-            @pl.when(here(i))
+            @pl.when(here(back_to(d)))
             def _():
                 local.start()
 
     for copy in fsdp_copies + grp_copies:
         copy.wait_send()
     gram_copy.wait_send()
-    for m in range(matrices):
+    for k in range(matrices):
         for h in range(2):
-            copy, mine = out_copy(m, h)
-            raw, _ = raw_copy(m, h)
+            copy, mine = out_copy(k, h)
+            raw, raw_mine = raw_copy(k, h)
+
+            @pl.when(jnp.logical_not(raw_mine))
+            def _():
+                raw.wait_send()
 
             @pl.when(jnp.logical_not(mine))
             def _():
-                raw.wait_send()
                 copy.wait_send()
 
     store_new.wait()
     for j in range(steps):
-        for i in range(size):
-            copy, local = back_copy(i, j)
-
-            @pl.when(jnp.logical_not(here(i)))
+        for d in range(size):
+            copy, local = back_copy(d, j)
+
+            @pl.when(jnp.logical_not(here(back_to(d))))
             def _():
                 copy.wait_send()
 
-            @pl.when(here(i))
+            @pl.when(here(back_to(d)))
             def _():
                 local.wait()
 

time: 50.4 us -> 49.6 us (0.984)
  the two profiles are of different devices: /device:TPU:24 before, /device:TPU:1 now
where the time goes in v7:
time: 49.6 us; the launch traced here: 49.5 us
  Pallas kernels  48.8 us (98%)
  between operations  0.64 us (1%)
    pallas_call x1, Pallas kernels, local(): pl.pallas_call(functools.partial(kernel, groups, size, paired), out_shape...  47.7 us
    pallas_call x1, Pallas kernels, local(): pl.pallas_call(store, out_shape=(jax.ShapeDtypeStruct(grads.shape, jnp.bf...  1.17 us

profile of v7, /device:TPU:1, one launch (start us, length us, event | category | flops | bytes accessed | tf_op | source)
XLA Modules:
  0.0 49.5 jit_solution(5096715078081495166)
XLA Ops:
  0.6 47.7 %shard_map.50 = (bf16[2,96,2048]{2,1,0:T(8,128)(2,1)S(1)}, bf16[2,96,2048]{2,1,0:T(8,128)(2,1)S(1)}) custom-call(s32[2]{0:T(128)} %counts_hbm.1, bf16[2,96,2048]{2,1,0:T(8,128)(2,1)} %grads_hbm.1, bf16[2,96,2048]{2,1,0:T(8,128)(2,1)} %momentum_hbm.1), custom_call_target="tpu_custom_call" | custom-call | flops 603979776 | bytes 3145728 | tf_op jit(solution)/shard_map/pallas_call | solution.py:376
  48.3 1.2 %shard_map.51 = (bf16[2,96,2048]{2,1,0:T(8,128)(2,1)}, bf16[2,96,2048]{2,1,0:T(8,128)(2,1)}) custom-call(bf16[2,96,2048]{2,1,0:T(8,128)(2,1)S(1)} %get-tuple-element.4.update, bf16[2,96,2048]{2,1,0:T(8,128)(2,1)S(1)} %get-tuple-element.5.new), custom_call_target="tpu_custom_call" | custom-call | tf_op jit(solution)/shard_map/pallas_call | solution.py:425

commit v8 on v7

--- a/solution.py
+++ b/solution.py
@@ -15,6 +15,7 @@
 ROW_STEP = 16
 SEND_COLS = 256
 RAW_COLS = 128
+GRAM_COLS = 256
 VMEM_BYTES = 40 * 1024 * 1024
 
 
@@ -46,9 +47,6 @@
 
         def target(m, h):
             return core * matrices + m, base + h
-
-        def nth(k):
-            return jnp.where(core == 1, matrices - 1 - k, k)
     else:
         owner_g = g
         owner_m = f // 2
@@ -58,17 +56,11 @@
         def target(m, h):
             return jnp.int32(2 * m + h), g
 
-        def nth(k):
-            return k
-
     barrier = pltpu.get_barrier_semaphore()
     others = [(lax.rem(f + d, size), g) for d in range(1, size)]
     others += [(f, lax.rem(g + d, groups)) for d in range(1, groups)]
     if paired:
         others += [(lax.rem(f + d, size), base + 1 - core) for d in range(1, size)]
-    for a, b in others:
-        pl.semaphore_signal(barrier, inc=1, device_id=dev(a, b), device_id_type=pl.DeviceIdType.MESH)
-
     load_counts = pltpu.make_async_copy(counts_hbm, counts_ref, count_sem)
     load_counts.start()
     piece = load_rows(rows)
@@ -83,7 +75,12 @@
         ]
         for k, (source, kept) in enumerate(((grads_hbm, grads), (momentum_hbm, momentum)))
     ]
-    for load in loads[0] + loads[1]:
+    for load in loads[0]:
+        load.start()
+    for a, b in others:
+        pl.semaphore_signal(barrier, inc=1, device_id=dev(a, b), device_id_type=pl.DeviceIdType.MESH)
+
+    for load in loads[1]:
         load.start()
 
     offset = f * rows
@@ -166,19 +163,17 @@
     row_total = total[8:9, 0:1]
     clip = jnp.minimum(1.0, lax.rsqrt(square_sum / (row_total * width) + 1e-06))
 
-    def out_copy(k, h):
-        m = nth(k)
+    def out_copy(m, h):
         a, b = target(m, h)
         copy = pltpu.make_async_remote_copy(
             fresh.at[m, :, pl.ds(h * half + RAW_COLS, half - RAW_COLS)],
             owned.at[pl.ds(pl.multiple_of(f * rows, 16), rows), pl.ds(RAW_COLS, half - RAW_COLS)],
-            out_send.at[k * 2 + h], out_recv.at[f],
+            out_send.at[m * 2 + h], out_recv.at[f],
             device_id=dev(a, b), device_id_type=pl.DeviceIdType.MESH,
         )
         return copy, jnp.logical_and(a == f, b == g)
 
-    for k in range(matrices):
-        m = nth(k)
+    for m in range(matrices):
         for h in range(2):
             cols = slice(h * half, (h + 1) * half)
             for r in range(0, rows, ROW_STEP):
@@ -188,7 +183,7 @@
                     0.95 * momentum[at].astype(jnp.float32) + clip * grads[at].astype(jnp.float32),
                     0.0,
                 ).astype(jnp.bfloat16)
-            copy, mine = out_copy(k, h)
+            copy, mine = out_copy(m, h)
 
             @pl.when(jnp.logical_not(mine))
             def _():
@@ -236,15 +231,25 @@
         return jnp.dot(a.astype(jnp.bfloat16), b.astype(jnp.bfloat16), preferred_element_type=jnp.float32)
 
     full = owned[...]
-    gram = lax.dot_general(full, full, (((1,), (1,)), ((), ())), preferred_element_type=jnp.float32)
-    gram_out[...] = gram.astype(jnp.bfloat16)
-    gram_copy = pltpu.make_async_remote_copy(
-        gram_out, gram_in, gram_send, gram_recv,
-        device_id=dev(*peer), device_id_type=pl.DeviceIdType.MESH,
-    )
-    gram_copy.start()
-    gram_copy.wait_recv()
-    gram = gram + gram_in[...].astype(jnp.float32)
+    slabs = []
+    for at, c in enumerate(range(0, full.shape[0], GRAM_COLS)):
+        cols = slice(c, min(c + GRAM_COLS, full.shape[0]))
+        part = lax.dot_general(
+            full, owned[cols, :], (((1,), (1,)), ((), ())), preferred_element_type=jnp.float32
+        )
+        gram_out[:, cols] = part.astype(jnp.bfloat16)
+        copy = pltpu.make_async_remote_copy(
+            gram_out.at[:, pl.ds(c, cols.stop - c)], gram_in.at[:, pl.ds(c, cols.stop - c)],
+            gram_send.at[at], gram_recv.at[at],
+            device_id=dev(*peer), device_id_type=pl.DeviceIdType.MESH,
+        )
+        copy.start()
+        slabs.append((copy, cols, part))
+    parts = []
+    for copy, cols, part in slabs:
+        copy.wait_recv()
+        parts.append(part + gram_in[:, cols].astype(jnp.float32))
+    gram = jnp.concatenate(parts, axis=1)
     order = gram.shape[0]
     diagonal = lax.broadcasted_iota(jnp.int32, (order, order), 0) == lax.broadcasted_iota(
         jnp.int32, (order, order), 1
@@ -304,18 +309,16 @@
 
     for copy in fsdp_copies + grp_copies:
         copy.wait_send()
-    gram_copy.wait_send()
-    for k in range(matrices):
+    for copy, _, _ in slabs:
+        copy.wait_send()
+    for m in range(matrices):
         for h in range(2):
-            copy, mine = out_copy(k, h)
-            raw, raw_mine = raw_copy(k, h)
-
-            @pl.when(jnp.logical_not(raw_mine))
+            copy, mine = out_copy(m, h)
+            raw, _ = raw_copy(m, h)
+
+            @pl.when(jnp.logical_not(mine))
             def _():
                 raw.wait_send()
-
-            @pl.when(jnp.logical_not(mine))
-            def _():
                 copy.wait_send()
 
     store_new.wait()
@@ -410,8 +413,8 @@
             dma((size,)),
             dma((2 * matrices,)),
             dma((size,)),
-            dma,
-            dma,
+            dma((-(-order // GRAM_COLS),)),
+            dma((-(-order // GRAM_COLS),)),
             dma((size * steps,)),
             dma((2 * matrices * steps,)),
         ],

time: 49.6 us -> 49.7 us (level)
  the two profiles are of different devices: /device:TPU:1 before, /device:TPU:24 now
where the time goes in v8:
time: 49.7 us; the launch traced here: 48.9 us
  Pallas kernels  48.3 us (97%)
  between operations  0.64 us (1%)
    pallas_call x1, Pallas kernels, local(): pl.pallas_call(functools.partial(kernel, groups, size, paired), out_shape...  47.1 us
    pallas_call x1, Pallas kernels, local(): pl.pallas_call(store, out_shape=(jax.ShapeDtypeStruct(grads.shape, jnp.bf...  1.17 us

profile of v8, /device:TPU:24, one launch (start us, length us, event | category | flops | bytes accessed | tf_op | source)
XLA Modules:
  0.0 48.9 jit_solution(12256888024570708473)
XLA Ops:
  0.6 47.1 %shard_map.50 = (bf16[2,96,2048]{2,1,0:T(8,128)(2,1)S(1)}, bf16[2,96,2048]{2,1,0:T(8,128)(2,1)S(1)}) custom-call(s32[2]{0:T(128)} %counts_hbm.1, bf16[2,96,2048]{2,1,0:T(8,128)(2,1)} %grads_hbm.1, bf16[2,96,2048]{2,1,0:T(8,128)(2,1)} %momentum_hbm.1), custom_call_target="tpu_custom_call" | custom-call | flops 603979776 | bytes 3145728 | tf_op jit(solution)/shard_map/pallas_call | solution.py:379
  47.7 1.2 %shard_map.51 = (bf16[2,96,2048]{2,1,0:T(8,128)(2,1)}, bf16[2,96,2048]{2,1,0:T(8,128)(2,1)}) custom-call(bf16[2,96,2048]{2,1,0:T(8,128)(2,1)S(1)} %get-tuple-element.4.update, bf16[2,96,2048]{2,1,0:T(8,128)(2,1)S(1)} %get-tuple-element.5.new), custom_call_target="tpu_custom_call" | custom-call | tf_op jit(solution)/shard_map/pallas_call | solution.py:428
